TPU v7x, 512 devices: a whole 4x4x16 slice. The times are simulated.
512 devices in a mesh: gx: 32 (over y, z_lo), ta: 16 (over z_hi, x, core).
Axes of the slice: x: 4, y: 4, z: 16 (z_hi: 2, z_lo: 8; z = z_hi * 8 + z_lo), core: 2. Of those that a mesh axis runs over, the one named last changes fastest.
Arguments:
- fields: float32 [5, 256, 512, 128], P(None, 'gx', 'ta'), may hold values from -6 to 6
- mean_axial: float32 [256, 128], P('gx'), may hold values from 0.1 to 0.9
- cycle_mean_density: float32 [128], replicated, may hold values from 0.6 to 1.4
- pml_layer: int32 [256, 128], P('gx'), may hold values from 0 to 12, as said below
- cycle_cutoff: int32 [16], replicated, may hold values from 1 to 64, as said below
Outputs:
- advanced: float32 [5, 256, 512, 128], P(None, 'gx', 'ta')
Inputs may be any that keep to these rules, and one draw needn't show every extreme that they name: The last entry of cycle_cutoff is 64. pml_layer is 0 in the interior and rises towards both axial ends and the outer radius, reaching 12 at the outermost cells.
All inputs are finite; a program needn't handle non-finite values.
Results may differ from a plain program's by a relative error of at most 0.00005.
Values sent between devices are 32-bit elements; how exact they have to be, the bound alone decides.
A program may use at most 64 MiB of HBM per device.

v0:
```python
import math

import jax
import jax.numpy as jnp
from jax import lax
from jax.sharding import PartitionSpec as P

NF = 16
PMLW = 12


coefs = (0.770882380518, -0.166705904415, 0.02084314277)
time_step = 0.1
damping_peak = 4.0


def with_halo(x, sides, width, wrap):
    for axis, dim in sides:
        peers, length = (lax.axis_size(axis), x.shape[dim])
        up = [(i, (i + 1) % peers) for i in range(peers if wrap else peers - 1)]
        down = [(j, i) for i, j in up]
        last = lax.slice_in_dim(x, length - width, length, axis=dim)
        initial = lax.slice_in_dim(x, 0, width, axis=dim)
        before = lax.ppermute(last, axis, up)
        after = lax.ppermute(initial, axis, down)
        x = jnp.concatenate([before, x, after], axis=dim)
    return x


def shifted(x, axis, by):
    peers = lax.axis_size(axis)
    return lax.ppermute(x, axis, [(i, (i + by) % peers) for i in range(peers)])


def derive(extended, axis, count):
    total = jnp.zeros_like(lax.slice_in_dim(extended, 3, 3 + count, axis=axis))
    for shift, weight in enumerate(coefs, 1):
        upper = lax.slice_in_dim(extended, 3 + shift, 3 + shift + count, axis=axis)
        lower = lax.slice_in_dim(extended, 3 - shift, 3 - shift + count, axis=axis)
        total = total + weight * (upper - lower)
    return total


def advance(
    fields, ext_x, ext_t, partner, mean_axial, cycle_mean_density, pml_layer, angular_spacing
):
    flips = jnp.array([1.0, 1.0, -1.0, -1.0, 1.0], jnp.float32).reshape(5, 1, 1, 1)
    ghost = (partner * flips)[..., ::-1]
    outside = jnp.zeros(fields.shape[:3] + (3,), jnp.float32)
    ext_r = jnp.concatenate([ghost, fields, outside], axis=3)
    axial_derivative_step = derive(ext_x, 1, fields.shape[1])
    angular_derivative_step = derive(ext_t, 2, fields.shape[2])
    radial_derivative_step = derive(ext_r, 3, fields.shape[3])
    radius = jnp.arange(fields.shape[3], dtype=jnp.float32) + 0.5
    inverse_radius = 1.0 / radius
    axial = mean_axial[:, None, :]
    dilatation = (
        axial_derivative_step[1]
        + radial_derivative_step[2]
        + fields[2] * inverse_radius
        + angular_derivative_step[3] * (inverse_radius / angular_spacing)
    )
    convection_term = axial * axial_derivative_step
    density_rate = -(convection_term[0] + cycle_mean_density * dilatation)
    rate_u = -(convection_term[1] + axial_derivative_step[4] / cycle_mean_density)
    rate_v = -(convection_term[2] + radial_derivative_step[4] / cycle_mean_density)
    rate_w = -(
        convection_term[3]
        + angular_derivative_step[4] * inverse_radius / (cycle_mean_density * angular_spacing)
    )
    pressure_rate = -(convection_term[4] + dilatation)
    rate = jnp.stack([density_rate, rate_u, rate_v, rate_w, pressure_rate])
    depth = pml_layer.astype(jnp.float32) / PMLW
    sigma = (damping_peak * depth * depth)[:, None, :]
    return fields + time_step * (rate - sigma * fields)


def spectral_tables(n_theta):
    half = n_theta // 2
    tindex = jnp.arange(n_theta, dtype=jnp.int32)
    mindex = jnp.arange(half, dtype=jnp.int32)
    phase = (tindex[:, None] * mindex[None, :] % n_theta).astype(jnp.float32) * (
        2.0 * math.pi / n_theta
    )
    weight = jnp.where(mindex == 0, 1.0 / n_theta, 2.0 / n_theta).astype(jnp.float32)
    return (jnp.cos(phase), jnp.sin(phase), weight, mindex)


def on_device(fields, mean_axial, cycle_mean_density, pml_layer, cycle_cutoff):
    sectors = lax.axis_size("ta")
    local_theta = fields.shape[2]
    n_theta = local_theta * sectors
    ext_x = with_halo(fields, (("gx", 1),), 3, False)
    ext_t = with_halo(fields, (("ta", 2),), 3, True)
    partner = shifted(fields[..., :3], "ta", sectors // 2)
    stepped = advance(
        fields,
        ext_x,
        ext_t,
        partner,
        mean_axial,
        cycle_mean_density,
        pml_layer,
        2.0 * math.pi / n_theta,
    )
    inner = jnp.moveaxis(stepped[..., :NF], 3, 0)
    cosines, sines, weight, mindex = spectral_tables(n_theta)
    highest = lax.Precision.HIGHEST
    piece = lax.all_gather(inner, "ta", axis=3, tiled=True)
    coef_cos = jnp.einsum("rfxt,tm->rfxm", piece, cosines, precision=highest)
    coef_sin = jnp.einsum("rfxt,tm->rfxm", piece, sines, precision=highest)
    keep = jnp.where(mindex[None, :] <= cycle_cutoff[:, None], weight[None, :], 0.0)
    cos_local = lax.dynamic_slice_in_dim(
        cosines, lax.axis_index("ta") * local_theta, local_theta, 0
    )
    sin_local = lax.dynamic_slice_in_dim(sines, lax.axis_index("ta") * local_theta, local_theta, 0)
    filtered = jnp.einsum(
        "rfxm,tm->rfxt", coef_cos * keep[:, None, None, :], cos_local, precision=highest
    )
    filtered = filtered + jnp.einsum(
        "rfxm,tm->rfxt", coef_sin * keep[:, None, None, :], sin_local, precision=highest
    )
    filtered = jnp.moveaxis(filtered, 0, 3)
    return jnp.concatenate([filtered, stepped[..., NF:]], axis=3)


def solution(mesh):
    return jax.shard_map(
        on_device,
        mesh=mesh,
        in_specs=(P(None, "gx", "ta", None), P("gx", None), P(), P("gx", None), P()),
        out_specs=P(None, "gx", "ta", None),
        check_vma=False,
    )
```

profile of v0, /device:TPU:97, one launch (start us, length us, event | category | flops | bytes accessed | tf_op | source)
XLA Modules:
  0.0 317.5 jit_solution(6133524353052712374)
XLA Ops:
  6.5 0.0 copy-start.1
  6.5 0.0 copy-start.2
  6.5 0.0 all-gather.2.cloned.1.call-start
  6.5 1.2 fusion.77
  7.7 4.8 %collective-permute-start.1 = (f32[5,3,32,128]{3,2,1,0:T(8,128)S(1)}, f32[5,3,32,128]{3,2,1,0:T(8,128)S(1)}, u32[]{:S(2)}, u32[]{:S(2)}) collective-permute-start(f32[5,3,32,128]{3,2,1,0:T(8,128)S(1)} %get-tuple-element.16), channel_id=1, source_target_pairs={{0,16},{16,32},{32,48},{48,64},{64,80},{80,96},{96,112},{112,128},... | collective-permute-start | bytes 737288 | tf_op jit(solution)/shard_map/ppermute | solution.py:24
  12.5 1.4 copy.17
  13.9 10.6 %collective-permute-start.2 = (f32[5,8,32,3]{2,1,3,0:T(8,128)S(1)}, f32[5,8,32,3]{2,1,3,0:T(8,128)S(1)}, u32[]{:S(2)}, u32[]{:S(2)}) collective-permute-start(f32[5,8,32,3]{2,1,3,0:T(8,128)S(1)} %copy.17), channel_id=1, source_target_pairs={{0,8},{1,9},{2,10},{3,11},{4,12},{5,13},{6,14},{7,15},{8,0},{9,1},... | collective-permute-start | bytes 46088 | tf_op jit(solution)/shard_map/ppermute | solution.py:32
  24.5 2.6 collective-permute-start
  27.1 1.0 fusion.76
  28.2 3.4 %collective-permute-start.3 = (f32[5,8,3,128]{3,2,1,0:T(4,128)S(1)}, f32[5,8,3,128]{3,2,1,0:T(4,128)S(1)}, u32[]{:S(2)}, u32[]{:S(2)}) collective-permute-start(f32[5,8,3,128]{3,2,1,0:T(4,128)S(1)} %get-tuple-element.13), channel_id=1, source_target_pairs={{1,0},{2,1},{3,2},{4,3},{5,4},{6,5},{7,6},{8,7},{9,8},{10,9},{11,1... | collective-permute-start | bytes 184328 | tf_op jit(solution)/shard_map/ppermute | solution.py:25
  31.6 3.0 collective-permute-start.4
  34.6 0.7 broadcast_multiply_fusion.2
  35.3 0.7 multiply_multiply_fusion
  36.0 0.0 collective-permute-done.2
  36.0 0.7 broadcast_multiply_fusion.1
  36.7 0.3 copy.9
  37.1 0.0 copy-start.3
  37.1 0.0 collective-permute-done.1
  37.1 4.7 %fusion.13 = (f32[5,8,32,128]{3,2,1,0:T(8,128)S(1)}, f32[5,8,35,128]{3,2,1,0:T(8,128)S(1)}, f32[5,11,32,128]{3,2,1,0:T(8,128)S(1)}, f32[5,11,32,128]{3,2,1,0:T(8,128)S(1)}) fusion(f32[5,8,32,3]{3,2,1,0:T(8,128)S(1)} %copy.9, f32[5,8,32,128]{3,2,1,0:T(8,128)} %param.6, f32[5,11,32,128]{3,2,1,0:T(8,128)S(1)} %constant_dynamic-update-slice_fusion.3), kind=kLoop, calls=%fused_computation.28 | loop fusion | flops 1802238 | bytes 3932160 | tf_op jit(solution)/shard_map/add | solution.py:40
  41.8 0.0 collective-permute-done
  41.9 0.9 broadcast_multiply_fusion
  42.8 0.0 collective-permute-done.3
  42.8 0.0 collective-permute-done.4
  42.8 0.0 copy-done.1
  42.8 0.5 fusion.5
  43.3 0.0 copy-done.2
  43.3 0.1 fusion.58
  43.5 0.1 multiply_add_fusion
  43.7 0.9 slice_bitcast_fusion
  44.6 0.0 all-gather.2.cloned.1.call-update
  44.6 1.9 fusion.40
  46.5 1.9 fusion.39
  48.4 0.0 copy-done.3
  48.4 0.1 fusion.63
  48.5 0.2 slice.195
  48.8 218.6 %all-gather.2.cloned.1.call-done = f32[16,5,8,512]{0,3,2,1:T(8,128)} async-done(((f32[16,5,8,32]{0,3,2,1:T(8,128)}), f32[16,5,8,512]{0,3,2,1:T(8,128)}) %all-gather.2.cloned.1.call-update) | async-done | bytes 1310736 | tf_op jit(solution)/shard_map/all_gather | solution.py:109
  267.4 0.0 copy-start
  267.4 22.0 %fusion.32 = f32[16,5,8,256]{3,0,2,1:T(8,128)S(1)} fusion(f32[16,5,8,512]{0,3,2,1:T(8,128)} %all-gather.2.cloned.1.call-done), kind=kOutput, calls=%fused_computation.57 | convolution fusion | flops 1008467968 | bytes 1966080 | tf_op jit(solution)/shard_map/rfxt,tm->rfxm/dot_general | solution.py:110
  289.4 1.0 fusion.26
  290.3 0.0 copy-done
  290.3 18.0 %fusion.30 = f32[16,5,8,256]{3,0,2,1:T(8,128)S(1)} fusion(f32[16,5,8,512]{0,3,2,1:T(8,128)S(1)} %copy-done), kind=kOutput, calls=%fused_computation.55 | convolution fusion | flops 1008467968 | bytes 1966080 | tf_op jit(solution)/shard_map/rfxt,tm->rfxm/dot_general | solution.py:111
  308.4 1.0 fusion
  309.3 0.3 copy.10
  309.6 1.1 pad_maximum_fusion.2
  (10 shorter events, 0.2 us)
Async XLA Ops:
  6.5 36.3 %copy-start.1 = (f32[5,8,32,128]{3,2,1,0:T(8,128)S(1)}, f32[5,8,32,128]{3,2,1,0:T(8,128)}, u32[]{:S(2)}) copy-start(f32[5,8,32,128]{3,2,1,0:T(8,128)} %param.6) | copy-start | bytes 1966084
  6.5 36.8 %copy-start.2 = (f32[128]{0:T(128)S(1)}, f32[128]{0:T(128)}, u32[]{:S(2)}) copy-start(f32[128]{0:T(128)} %param.8) | copy-start | bytes 1540
  6.5 260.9 %all-gather.2.cloned.1.call-start = ((), (), s32[]{:S(2)}) async-start(), calls=%async_computation | async-start | bytes 11141120 | tf_op jit(solution)/shard_map/all_gather | solution.py:109
  7.7 29.4 %collective-permute-start.1 = (f32[5,3,32,128]{3,2,1,0:T(8,128)S(1)}, f32[5,3,32,128]{3,2,1,0:T(8,128)S(1)}, u32[]{:S(2)}, u32[]{:S(2)}) collective-permute-start(f32[5,3,32,128]{3,2,1,0:T(8,128)S(1)} %get-tuple-element.16), channel_id=1, source_target_pairs={{0,16},{16,32},{32,48},{48,64},{64,80},{80,96},{96,112},{112,128},... | collective-permute-start | bytes 737288 | tf_op jit(solution)/shard_map/ppermute | solution.py:24
  13.9 22.1 %collective-permute-start.2 = (f32[5,8,32,3]{2,1,3,0:T(8,128)S(1)}, f32[5,8,32,3]{2,1,3,0:T(8,128)S(1)}, u32[]{:S(2)}, u32[]{:S(2)}) collective-permute-start(f32[5,8,32,3]{2,1,3,0:T(8,128)S(1)} %copy.17), channel_id=1, source_target_pairs={{0,8},{1,9},{2,10},{3,11},{4,12},{5,13},{6,14},{7,15},{8,0},{9,1},... | collective-permute-start | bytes 46088 | tf_op jit(solution)/shard_map/ppermute | solution.py:32
  24.5 17.3 %collective-permute-start = (f32[5,3,32,128]{3,2,1,0:T(8,128)S(1)}, f32[5,3,32,128]{3,2,1,0:T(8,128)S(1)}, u32[]{:S(2)}, u32[]{:S(2)}) collective-permute-start(f32[5,3,32,128]{3,2,1,0:T(8,128)S(1)} %get-tuple-element.15), channel_id=1, source_target_pairs={{16,0},{32,16},{48,32},{64,48},{80,64},{96,80},{112,96},{128,112},... | collective-permute-start | bytes 737288 | tf_op jit(solution)/shard_map/ppermute | solution.py:25
  28.2 14.6 %collective-permute-start.3 = (f32[5,8,3,128]{3,2,1,0:T(4,128)S(1)}, f32[5,8,3,128]{3,2,1,0:T(4,128)S(1)}, u32[]{:S(2)}, u32[]{:S(2)}) collective-permute-start(f32[5,8,3,128]{3,2,1,0:T(4,128)S(1)} %get-tuple-element.13), channel_id=1, source_target_pairs={{1,0},{2,1},{3,2},{4,3},{5,4},{6,5},{7,6},{8,7},{9,8},{10,9},{11,1... | collective-permute-start | bytes 184328 | tf_op jit(solution)/shard_map/ppermute | solution.py:25
  31.6 11.2 %collective-permute-start.4 = (f32[5,8,3,128]{3,2,1,0:T(4,128)S(1)}, f32[5,8,3,128]{3,2,1,0:T(4,128)S(1)}, u32[]{:S(2)}, u32[]{:S(2)}) collective-permute-start(f32[5,8,3,128]{3,2,1,0:T(4,128)S(1)} %get-tuple-element.14), channel_id=1, source_target_pairs={{0,1},{1,2},{2,3},{3,4},{4,5},{5,6},{6,7},{7,8},{8,9},{9,10},{10,1... | collective-permute-start | bytes 184328 | tf_op jit(solution)/shard_map/ppermute | solution.py:24
  37.1 11.4 %copy-start.3 = (s32[16]{0:T(128)S(1)}, s32[16]{0:T(128)}, u32[]{:S(2)}) copy-start(s32[16]{0:T(128)} %param.10) | copy-start | bytes 196
  267.4 22.9 %copy-start = (f32[16,5,8,512]{0,3,2,1:T(8,128)S(1)}, f32[16,5,8,512]{0,3,2,1:T(8,128)}, u32[]{:S(2)}) copy-start(f32[16,5,8,512]{0,3,2,1:T(8,128)} %all-gather.2.cloned.1.call-done) | copy-start | bytes 3932164
Sparse Core Ops, SparseCore 0:
  44.7 222.6 all-gather.1
where the time goes:
time: 318 us
  waiting for transfers between devices  219 us (69%)
  matrix products  41.9 us (13%)
  starting transfers between devices  24.5 us (8%)
  between operations  13.6 us (4%)
  other arithmetic  13.5 us (4%)
  local copies, waits for them, and re-layouts  5.36 us (2%)
    all_gather x1, waiting for transfers between devices, on_device(): piece = lax.all_gather(inner, 'ta', axis=3, tiled=True)  219 us
    dot_general x1, matrix products, on_device(): coef_cos = jnp.einsum('rfxt,tm->rfxm', piece, cosines, precision=highest)  22 us
    dot_general x1, matrix products, on_device(): coef_sin = jnp.einsum('rfxt,tm->rfxm', piece, sines, precision=highest)  18 us
    ppermute x1, starting transfers between devices, shifted(): return lax.ppermute(x, axis, [(i, (i + by) % peers) for i in range(peers)])  10.6 us
    ppermute x2, starting transfers between devices, with_halo(): before = lax.ppermute(last, axis, up)  7.77 us
  transfers between devices with their start and end apart: 6, of which 1 were waited for; matrix products, arithmetic and copies ran while one was open for 5% of the time, Pallas kernels for 0%

commit v1 on v0

v1 whole, which is shorter than its diff:
```python
import functools
import math

import jax
import jax.numpy as jnp
import numpy as np
from jax import lax
from jax.experimental import pallas as pl
from jax.experimental.pallas import tpu as pltpu
from jax.sharding import PartitionSpec as P

NF = 16
PMLW = 12
MODES = 64
LANES = 128

A1, A2, A3 = 0.770882380518, -0.166705904415, 0.020843142770
DT = 0.1
PEAK = 4.0
F32 = jnp.float32
MESH = pl.DeviceIdType.MESH


def left(x, by):
    return pltpu.roll(x, LANES - by, x.ndim - 1)


def right(x, by):
    return pltpu.roll(x, by, x.ndim - 1)


def periodic(x, lane):
    x = jnp.where(lane < NF, x, 0.0)
    x = x + right(x, 16)
    x = x + right(x, 32)
    return x + right(x, 64)


def group(lane, g):
    return (lane >= NF * g) & (lane < NF * (g + 1))


def body(
    n_gx, n_ta, spacing,
    fields, mean, dens, pml, cut, forward, inverse, out,
    fx, ext, rx, ex, zr, dp, qs, gr, th_out, th_in, ps, pr, bs, br, mt, st, sg,
    load_sem, ring_send, ring_recv, th_send, th_recv, rx_send, rx_recv,
    a_send, a_recv, z_send, z_recv, b_send, b_recv,
):
    half = n_ta // 2
    gx = lax.axis_index("gx")
    ta = lax.axis_index("ta")
    k = lax.rem(ta, half)
    base = ta - k
    partner = lax.rem(ta + half, n_ta)
    after = lax.rem(ta + 1, n_ta)
    before = lax.rem(ta + n_ta - 1, n_ta)
    has_low = gx > 0
    has_high = gx < n_gx - 1
    low = jnp.maximum(gx - 1, 0)
    high = jnp.minimum(gx + 1, n_gx - 1)
    edge_low = k == 0
    edge_high = k == half - 1
    mates = [base + lax.rem(k + i, half) for i in range(1, half)]

    barrier = pltpu.get_barrier_semaphore()

    def greet(**where):
        pl.semaphore_signal(barrier, inc=1, device_id=where, device_id_type=MESH)

    for mate in mates:
        greet(ta=mate)
    greet(ta=partner)
    pl.when(has_low)(lambda: greet(gx=low))
    pl.when(has_high)(lambda: greet(gx=high))
    pl.when(edge_low)(lambda: greet(ta=before))
    pl.when(edge_high)(lambda: greet(ta=after))

    load = pltpu.make_async_copy(fields, fx.at[:, 3:11], load_sem.at[0])
    load.start()
    load_t = pltpu.make_async_copy(fields.at[3:5], ext.at[:, :, 8:40], load_sem.at[1])
    load_t.start()

    lane = lax.broadcasted_iota(jnp.int32, (1, LANES), 1)
    lane8 = lax.broadcasted_iota(jnp.int32, (8, LANES), 1)
    inv_r = 1.0 / (lane.astype(F32) + 0.5)
    inv_dt = 1.0 / spacing
    rho0 = dens[...]
    depth = pml[...].astype(F32) / PMLW
    damp = 1.0 - DT * (PEAK * depth * depth)
    st[...] = damp
    mt[...] = periodic(mean[...], lane8)
    sg[...] = periodic(damp, lane8)
    rho0_p = periodic(jnp.broadcast_to(rho0, (8, LANES)), lane8)[0:1]
    inv_r_p = periodic(jnp.broadcast_to(inv_r, (8, LANES)), lane8)[0:1]

    def on(g, value):
        return jnp.where(group(lane, g), value, 0.0)

    up_w = [jnp.where(lane < LANES - s, a, 0.0) for s, a in ((1, A1), (2, A2), (3, A3))]
    dn_w = [jnp.where(lane >= s, a, 0.0) for s, a in ((1, A1), (2, A2), (3, A3))]
    g_0 = jnp.where(lane == 0, A1, jnp.where(lane == 1, A3, 0.0))
    g_u1 = jnp.where(lane == 0, A2, 0.0)
    g_u2 = jnp.where(lane == 0, A3, 0.0)
    g_d1 = jnp.where(lane == 1, A2, 0.0)
    g_d2 = jnp.where(lane == 2, A3, 0.0)
    c_e = on(0, -DT * rho0_p) + on(2, -DT / rho0_p) + on(4, -DT)

    def radial(f):
        ups = [left(f, s) for s in (1, 2, 3)]
        dns = [right(f, s) for s in (1, 2, 3)]
        d = (up_w[0] * ups[0] - dn_w[0] * dns[0]) + (up_w[1] * ups[1] - dn_w[1] * dns[1])
        d = d + (up_w[2] * ups[2] - dn_w[2] * dns[2])
        ghost = g_0 * f + g_u1 * ups[0] + g_u2 * ups[1] + g_d1 * dns[0] + g_d2 * dns[1]
        return d, ghost

    load.wait()
    load_t.wait()

    def pack(x, carry):
        rho, u, v, w, p = (fx[f, 3 + x] for f in range(5))
        dv, gv = radial(v)
        dpr, gp = radial(p)
        z = dv + v * inv_r
        zr[x] = z
        dp[x] = dpr
        r = jnp.where(lane < 96, right(w, 80), jnp.where(lane < 112, right(p, 96), right(gv, 112) + right(gp, 115)))
        r = jnp.where(lane < 80, right(p, 64), r)
        r = jnp.where(lane < 64, right(w, 48), r)
        r = jnp.where(lane < 48, right(v, 32), r)
        r = jnp.where(lane < 32, right(u, 16), r)
        r = jnp.where(lane < 16, rho, r)
        rx[3 + x] = r
        e = jnp.where(lane < 16, z, jnp.where(lane < 48, right(dpr, 32), right(z, 64)))
        ex[x] = e * c_e
        for f in range(2):
            th_out[0, x, 3 * f : 3 * f + 3] = ext[f, x, 8:11]
            th_out[1, x, 3 * f : 3 * f + 3] = ext[f, x, 37:40]
        return carry

    th_out[...] = jnp.zeros_like(th_out)
    lax.fori_loop(0, 8, pack, 0)

    pl.semaphore_wait(
        barrier,
        half + has_low.astype(jnp.int32) + has_high.astype(jnp.int32) + edge_low.astype(jnp.int32) + edge_high.astype(jnp.int32),
    )

    def remote(src, dst, send, recv, **where):
        return pltpu.make_async_remote_copy(
            src_ref=src, dst_ref=dst, send_sem=send, recv_sem=recv, device_id=where, device_id_type=MESH
        )

    rx_up = remote(rx.at[8:11], rx.at[0:3], rx_send.at[0], rx_recv.at[0], gx=high)
    rx_down = remote(rx.at[3:6], rx.at[11:14], rx_send.at[1], rx_recv.at[1], gx=low)
    fx_up = remote(fx.at[:, 8:11], fx.at[:, 0:3], ring_send.at[0], ring_recv.at[0], gx=high)
    fx_down = remote(fx.at[:, 3:6], fx.at[:, 11:14], ring_send.at[1], ring_recv.at[1], gx=low)
    th_down = remote(th_out.at[0], th_in.at[1], th_send.at[0], th_recv.at[1], ta=before)
    th_up = remote(th_out.at[1], th_in.at[0], th_send.at[1], th_recv.at[0], ta=after)

    pl.when(has_high)(rx_up.start)
    pl.when(has_low)(rx_down.start)
    th_down.start()
    th_up.start()
    pl.when(has_high)(fx_up.start)
    pl.when(has_low)(fx_down.start)

    @pl.when(jnp.logical_not(has_low))
    def _():
        rx[0:3] = jnp.zeros((3,) + rx.shape[1:], F32)
        fx[:, 0:3] = jnp.zeros((5, 3) + fx.shape[2:], F32)

    @pl.when(jnp.logical_not(has_high))
    def _():
        rx[11:14] = jnp.zeros((3,) + rx.shape[1:], F32)
        fx[:, 11:14] = jnp.zeros((5, 3) + fx.shape[2:], F32)

    c_a = on(0, -DT * rho0_p)
    c_b = on(1, -DT / rho0_p)
    c_c = on(4, -DT)

    pl.when(has_low)(rx_up.wait_recv)
    pl.when(has_high)(rx_down.wait_recv)

    def step_inner(x, carry):
        d = A1 * (rx[4 + x] - rx[2 + x]) + A2 * (rx[5 + x] - rx[1 + x]) + A3 * (rx[6 + x] - rx[x])
        r = rx[3 + x]
        row = pl.ds(x, 1)
        s = r * sg[row] - (DT * mt[row]) * d + ex[x]
        s = s + c_a * left(d, 16) + c_b * left(d, 48) + c_c * right(d, 48)
        qs[x] = jnp.where(lane < 80, s, r)
        return carry

    lax.fori_loop(0, 8, step_inner, 0)

    a_copies = []
    for i in range(1, half):
        there = lax.rem(k + i, half)
        copy = remote(qs.at[there], gr.at[k], a_send.at[i - 1], a_recv.at[i - 1], ta=base + there)
        copy.start()
        a_copies.append(copy)
    gr[k] = qs[k]

    th_up.wait_recv()
    th_down.wait_recv()
    damp_rho = -DT * rho0
    damp_v = -DT / rho0

    def local_part(x, carry):
        for f in range(2):
            ext[f, x, 5:8] = th_in[0, x, 3 * f : 3 * f + 3]
            ext[f, x, 40:43] = th_in[1, x, 3 * f : 3 * f + 3]

        def angular(f):
            d = A1 * (ext[f, x, 9:41] - ext[f, x, 7:39]) + A2 * (ext[f, x, 10:42] - ext[f, x, 6:38])
            return d + A3 * (ext[f, x, 11:43] - ext[f, x, 5:37])

        keep = st[pl.ds(x, 1)]
        around = inv_r * inv_dt
        z = zr[x] + angular(0) * around
        out[0, x] = fx[0, 3 + x] * keep + damp_rho * z
        out[1, x] = fx[1, 3 + x] * keep
        out[2, x] = fx[2, 3 + x] * keep + damp_v * dp[x]
        out[3, x] = fx[3, 3 + x] * keep + damp_v * (angular(1) * around)
        out[4, x] = fx[4, 3 + x] * keep - DT * z
        return carry

    lax.fori_loop(0, 8, local_part, 0)

    for copy in a_copies:
        copy.wait()
    g = gr[...].reshape(8 * gr.shape[1], LANES)
    highest = lax.Precision.HIGHEST
    coef = jnp.dot(forward[...], g, precision=highest, preferred_element_type=F32)
    zero_mode = jnp.sum(g, axis=0, keepdims=True)
    a_m, b_m = coef[:MODES], coef[MODES:]
    kappa = 2.0 * (A1 * forward[MODES:, 1:2] + A2 * forward[MODES:, 2:3] + A3 * forward[MODES:, 3:4])
    row = lax.broadcasted_iota(jnp.int32, (MODES, LANES), 0)
    sign = jnp.where(lax.rem(row, 2) == 1, 1.0, -1.0)
    around_p = -DT * inv_r_p * inv_dt
    t_r, t_p, t_w = on(0, around_p * rho0_p), on(4, around_p), on(3, around_p / rho0_p)
    three = lane < 3
    h_r = jnp.where(three, -DT * rho0_p, 0.0)
    h_p = jnp.where((lane >= 64) & (lane < 67), -DT, 0.0)
    h_v = jnp.where((lane >= 32) & (lane < 35), DT / rho0_p, 0.0)

    def turned(c):
        return t_r * left(c, 80) + t_p * left(c, 16) + t_w * left(c, 48)

    def mirrored(c):
        return h_r * left(c, 112) + h_p * left(c, 48) + h_v * left(c, 83)

    new_a = a_m + turned(kappa * b_m) + sign * mirrored(a_m)
    new_b = b_m - turned(kappa * a_m) + sign * mirrored(b_m)
    zero8 = jnp.broadcast_to(zero_mode, (8, LANES))
    zero8 = zero8 + mirrored(zero8)

    for h, c in ((0, new_a), (1, new_b)):
        t5, t6, t7 = c[40:48], c[48:56], c[56:64]
        for i in range(5):
            spread = jnp.where(lane < 112, right(t6, 96 - 16 * i), right(t7, 112 - 16 * i))
            spread = jnp.where(lane < 96, right(t5, 80 - 16 * i), spread)
            ps[5 * h + i] = jnp.where(lane < 80, c[8 * i : 8 * i + 8], spread)
    ps[10] = zero8
    across = remote(ps, pr, z_send, z_recv, ta=partner)
    across.start()
    cuts = jnp.concatenate([cut[...]] * 8, axis=1)
    keep = jnp.where(row + 1 <= cuts, 2.0 / (n_ta * gr.shape[1]), 0.0)
    across.wait()

    total = []
    for h, c in ((0, new_a), (1, new_b)):
        parts = [pr[5 * h + i] for i in range(5)]
        tiles = list(parts)
        for first in (80, 96, 112):
            tile = left(parts[0], first)
            for i in range(1, 5):
                tile = jnp.where(lane < 16 * i, tile, left(parts[i], first - 16 * i))
            tiles.append(tile)
        total.append((c + sign * jnp.concatenate(tiles, axis=0)) * keep)
    both = jnp.concatenate(total, axis=0)
    mean_mode = (zero8 + pr[10])[0:1] * (1.0 / (n_ta * gr.shape[1]))
    filtered = jnp.dot(inverse[...], both, precision=highest, preferred_element_type=F32) + mean_mode
    bs[...] = filtered.reshape(bs.shape)

    b_copies = []
    for i in range(1, half):
        there = lax.rem(k + i, half)
        copy = remote(bs.at[there], br.at[k], b_send.at[i - 1], b_recv.at[i - 1], ta=base + there)
        copy.start()
        b_copies.append(copy)
    br[k] = bs[k]

    pl.when(has_low)(fx_up.wait_recv)
    pl.when(has_high)(fx_down.wait_recv)
    inv_rho0 = 1.0 / rho0

    def axial_part(x, carry):
        def axial(f):
            d = A1 * (fx[f, 4 + x] - fx[f, 2 + x]) + A2 * (fx[f, 5 + x] - fx[f, 1 + x])
            return d + A3 * (fx[f, 6 + x] - fx[f, x])

        along = DT * mean[pl.ds(x, 1)]
        d_u, d_p = axial(1), axial(4)
        out[0, x] = out[0, x] - along * axial(0) + damp_rho * d_u
        out[1, x] = out[1, x] - along * d_u + damp_v * d_p
        out[2, x] = out[2, x] - along * axial(2)
        out[3, x] = out[3, x] - along * axial(3)
        out[4, x] = out[4, x] - along * d_p - DT * d_u
        return carry

    lax.fori_loop(0, 8, axial_part, 0)

    for copy in b_copies:
        copy.wait()

    def merge(x, carry):
        t = br[x]
        for f in range(5):
            out[f, x] = jnp.where(lane < NF, left(t, 16 * f) if f else t, out[f, x])
        return carry

    lax.fori_loop(0, 8, merge, 0)

    pl.when(has_high)(rx_up.wait_send)
    pl.when(has_low)(rx_down.wait_send)
    pl.when(has_high)(fx_up.wait_send)
    pl.when(has_low)(fx_down.wait_send)
    th_down.wait_send()
    th_up.wait_send()


def tables(points, n_theta):
    n = np.arange(points)
    m = np.arange(1, MODES + 1)
    phase = (m[:, None] * n[None, :] % n_theta) * (2.0 * math.pi / n_theta)
    forward = np.concatenate([np.cos(phase), np.sin(phase)]).astype(np.float32)
    return forward, np.ascontiguousarray(forward.T)


def solution(mesh):
    n_gx, n_ta = mesh.shape["gx"], mesh.shape["ta"]

    def on_device(fields, mean_axial, cycle_mean_density, pml_layer, cycle_cutoff):
        nf, nx, nt, nr = fields.shape
        n_theta = nt * n_ta
        forward, inverse = tables(n_theta // 2, n_theta)
        vmem = pl.BlockSpec(memory_space=pltpu.VMEM)
        half = n_ta // 2
        dma = pltpu.SemaphoreType.DMA
        return pl.pallas_call(
            functools.partial(body, n_gx, n_ta, 2.0 * math.pi / n_theta),
            out_shape=jax.ShapeDtypeStruct(fields.shape, F32),
            in_specs=[pl.BlockSpec(memory_space=pl.ANY)] + [vmem] * 6,
            out_specs=vmem,
            scratch_shapes=[
                pltpu.VMEM((nf, nx + 6, nt, nr), F32),
                pltpu.VMEM((2, nx, nt + 16, nr), F32),
                pltpu.VMEM((nx + 6, nt, nr), F32),
                pltpu.VMEM((nx, nt, nr), F32),
                pltpu.VMEM((nx, nt, nr), F32),
                pltpu.VMEM((nx, nt, nr), F32),
                pltpu.VMEM((nx, nt, nr), F32),
                pltpu.VMEM((nx, nt, nr), F32),
                pltpu.VMEM((2, nx, 8, nr), F32),
                pltpu.VMEM((2, nx, 8, nr), F32),
                pltpu.VMEM((11, 8, nr), F32),
                pltpu.VMEM((11, 8, nr), F32),
                pltpu.VMEM((nx, nt, nr), F32),
                pltpu.VMEM((nx, nt, nr), F32),
                pltpu.VMEM((nx, nr), F32),
                pltpu.VMEM((nx, nr), F32),
                pltpu.VMEM((nx, nr), F32),
                dma((2,)),
                dma((2,)), dma((2,)),
                dma((2,)), dma((2,)),
                dma((2,)), dma((2,)),
                dma((half - 1,)), dma((half - 1,)),
                dma, dma,
                dma((half - 1,)), dma((half - 1,)),
            ],
            compiler_params=pltpu.CompilerParams(
                collective_id=0, has_side_effects=True, vmem_limit_bytes=16 * 1024 * 1024
            ),
        )(
            fields,
            mean_axial,
            cycle_mean_density.reshape(1, nr),
            pml_layer,
            cycle_cutoff.reshape(1, NF),
            jnp.asarray(forward),
            jnp.asarray(inverse),
        )

    return jax.shard_map(
        on_device,
        mesh=mesh,
        in_specs=(P(None, "gx", "ta", None), P("gx", None), P(), P("gx", None), P()),
        out_specs=P(None, "gx", "ta", None),
        check_vma=False,
    )
```

time: 318 us -> 48.7 us (0.15)
  the two profiles are of different devices: /device:TPU:97 before, /device:TPU:24 now
where the time goes in v1:
time: 48.7 us; the launch traced here: 48.2 us
  Pallas kernels  42.4 us (87%)
  local copies, waits for them, and re-layouts  5.78 us (12%)
    pallas_call x1, Pallas kernels, on_device(): pl.pallas_call(functools.partial(body, n_gx, n_ta, 2.0 * math.pi / n_thet...  42.4 us
    unnamed x15, local copies, waits for them, and re-layouts  5.78 us

profile of v1, /device:TPU:24, one launch (start us, length us, event | category | flops | bytes accessed | tf_op | source)
XLA Modules:
  0.0 48.2 jit_solution(12661398399385946705)
XLA Ops:
  0.0 0.0 copy-start.5
  0.0 0.0 copy-start.6
  0.0 0.7 %copy-done.5 = f32[128]{0:T(128)S(1)} copy-done((f32[128]{0:T(128)S(1)}, f32[128]{0:T(128)}, u32[]{:S(2)}) %copy-start.5) | copy-done | bytes 536
  0.7 0.0 copy-done.6
  0.7 0.0 copy-start
  0.7 1.1 %copy-done = f32[5,8,32,128]{3,2,1,0:T(8,128)S(1)} copy-done((f32[5,8,32,128]{3,2,1,0:T(8,128)S(1)}, f32[5,8,32,128]{3,2,1,0:T(8,128)}, u32[]{:S(2)}) %copy-start) | copy-done | bytes 655384
  1.8 0.0 copy-start.1
  1.8 0.9 %copy-done.1 = f32[256,128]{1,0:T(8,128)S(1)} copy-done((f32[256,128]{1,0:T(8,128)S(1)}, f32[256,128]{1,0:T(8,128)}, u32[]{:S(2)}) %copy-start.1) | copy-done | bytes 131096
  2.7 0.0 copy-start.2
  2.7 0.9 %copy-done.2 = f32[128,256]{1,0:T(8,128)S(1)} copy-done((f32[128,256]{1,0:T(8,128)S(1)}, f32[128,256]{1,0:T(8,128)}, u32[]{:S(2)}) %copy-start.2) | copy-done | bytes 131096
  3.6 0.0 copy-start.3
  3.6 0.7 %copy-done.3 = f32[8,128]{1,0:T(8,128)S(1)} copy-done((f32[8,128]{1,0:T(8,128)S(1)}, f32[8,128]{1,0:T(8,128)}, u32[]{:S(2)}) %copy-start.3) | copy-done | bytes 4120
  4.3 0.0 copy-start.4
  4.3 0.7 %copy-done.4 = s32[8,128]{1,0:T(8,128)S(1)} copy-done((s32[8,128]{1,0:T(8,128)S(1)}, s32[8,128]{1,0:T(8,128)}, u32[]{:S(2)}) %copy-start.4) | copy-done | bytes 4120
  4.9 42.4 %shard_map.73 = f32[5,8,32,128]{3,2,1,0:T(8,128)S(1)} custom-call(f32[5,8,32,128]{3,2,1,0:T(8,128)S(1)} %copy-done, f32[8,128]{1,0:T(8,128)S(1)} %copy-done.3, f32[1,128]{1,0:T(1,128)S(1)} %bitcast.2, s32[8,128]{1,0:T(8,128)S(1)} %copy-done.4, s32[1,16]{1,0:T(1,128)S(1)} %bitcast.3, f32[128,256]{1,0:T(8,128)S(1)} %copy-done.2, f32[256,128]{1,0:T(8,128)S(1)} %copy-done.1), custom_call_target="tpu_custom_call" | custom-call | tf_op jit(solution)/shard_map/pallas_call | solution.py:351
  47.3 0.8 %copy.9 = f32[5,8,32,128]{3,2,1,0:T(8,128)} copy(f32[5,8,32,128]{3,2,1,0:T(8,128)S(1)} %shard_map.73) | data formatting | bytes 1310720
Async XLA Ops:
  0.0 0.7 %copy-start.5 = (f32[128]{0:T(128)S(1)}, f32[128]{0:T(128)}, u32[]{:S(2)}) copy-start(f32[128]{0:T(128)} %param.9) | copy-start | bytes 1540
  0.0 0.7 %copy-start.6 = (s32[16]{0:T(128)S(1)}, s32[16]{0:T(128)}, u32[]{:S(2)}) copy-start(s32[16]{0:T(128)} %param.11) | copy-start | bytes 196
  0.7 1.1 %copy-start = (f32[5,8,32,128]{3,2,1,0:T(8,128)S(1)}, f32[5,8,32,128]{3,2,1,0:T(8,128)}, u32[]{:S(2)}) copy-start(f32[5,8,32,128]{3,2,1,0:T(8,128)} %fields.1) | copy-start | bytes 1966084
  1.8 0.9 %copy-start.1 = (f32[256,128]{1,0:T(8,128)S(1)}, f32[256,128]{1,0:T(8,128)}, u32[]{:S(2)}) copy-start(f32[256,128]{1,0:T(8,128)} %constant.5.clone.inverse) | copy-start | bytes 393220
  2.7 0.9 %copy-start.2 = (f32[128,256]{1,0:T(8,128)S(1)}, f32[128,256]{1,0:T(8,128)}, u32[]{:S(2)}) copy-start(f32[128,256]{1,0:T(8,128)} %constant.4.clone.forward) | copy-start | bytes 393220
  3.6 0.7 %copy-start.3 = (f32[8,128]{1,0:T(8,128)S(1)}, f32[8,128]{1,0:T(8,128)}, u32[]{:S(2)}) copy-start(f32[8,128]{1,0:T(8,128)} %mean.1) | copy-start | bytes 12292
  4.3 0.7 %copy-start.4 = (s32[8,128]{1,0:T(8,128)S(1)}, s32[8,128]{1,0:T(8,128)}, u32[]{:S(2)}) copy-start(s32[8,128]{1,0:T(8,128)} %pml.1) | copy-start | bytes 12292

commit v2 on v1

--- a/solution.py
+++ b/solution.py
@@ -42,11 +42,18 @@
 
 def body(
     n_gx, n_ta, spacing,
-    fields, mean, dens, pml, cut, forward, inverse, out,
-    fx, ext, rx, ex, zr, dp, qs, gr, th_out, th_in, ps, pr, bs, br, mt, st, sg,
-    load_sem, ring_send, ring_recv, th_send, th_recv, rx_send, rx_recv,
-    a_send, a_recv, z_send, z_recv, b_send, b_recv,
+    fields, *rest,
 ):
+    inputs, rest = rest[:6], rest[6:]
+    out, rest = rest[0], rest[1:]
+    local, rest = rest[:6], rest[6:]
+    input_sem, rest = rest[0], rest[1:]
+    mean, dens, pml, cut, forward, inverse = local
+    (
+    fx, ext, rx, ex, zr, dp, qs, gr, hs, hr, th_out, th_in, ps, pr, bs, br, mt, st, sg,
+    load_sem, ring_send, ring_recv, th_send, th_recv, h_send, h_recv,
+    a_send, a_recv, z_send, z_recv, b_send, b_recv, far,
+    ) = rest
     half = n_ta // 2
     gx = lax.axis_index("gx")
     ta = lax.axis_index("ta")
@@ -61,25 +68,44 @@
     high = jnp.minimum(gx + 1, n_gx - 1)
     edge_low = k == 0
     edge_high = k == half - 1
+    second = ta >= half
     mates = [base + lax.rem(k + i, half) for i in range(1, half)]
+    takes_low = k < 3
+    takes_high = k > half - 4
 
     barrier = pltpu.get_barrier_semaphore()
 
-    def greet(**where):
-        pl.semaphore_signal(barrier, inc=1, device_id=where, device_id_type=MESH)
+    def greet(sem, **where):
+        pl.semaphore_signal(sem, inc=1, device_id=where, device_id_type=MESH)
+
+    def greet_across(sem):
+        greet(sem, ta=partner)
+        pl.when(edge_low)(lambda: greet(sem, ta=before))
+        pl.when(edge_high)(lambda: greet(sem, ta=after))
 
     for mate in mates:
-        greet(ta=mate)
-    greet(ta=partner)
-    pl.when(has_low)(lambda: greet(gx=low))
-    pl.when(has_high)(lambda: greet(gx=high))
-    pl.when(edge_low)(lambda: greet(ta=before))
-    pl.when(edge_high)(lambda: greet(ta=after))
+        greet(barrier, ta=mate)
+    pl.when(jnp.logical_not(second))(lambda: greet_across(barrier))
+    for exists, takes, there in ((has_low, takes_low, low), (has_high, takes_high, high)):
+
+        @pl.when(exists)
+        def _():
+            greet(barrier, gx=there)
+
+            @pl.when(takes)
+            def _():
+                for mate in mates:
+                    greet(barrier, gx=there, ta=mate)
 
     load = pltpu.make_async_copy(fields, fx.at[:, 3:11], load_sem.at[0])
     load.start()
     load_t = pltpu.make_async_copy(fields.at[3:5], ext.at[:, :, 8:40], load_sem.at[1])
     load_t.start()
+    small = [pltpu.make_async_copy(inputs[i], local[i], input_sem.at[i]) for i in range(6)]
+    for copy in small:
+        copy.start()
+    for copy in small[:4]:
+        copy.wait()
 
     lane = lax.broadcasted_iota(jnp.int32, (1, LANES), 1)
     lane8 = lax.broadcasted_iota(jnp.int32, (8, LANES), 1)
@@ -139,60 +165,69 @@
         return carry
 
     th_out[...] = jnp.zeros_like(th_out)
+    rx[0:3] = jnp.zeros((3,) + rx.shape[1:], F32)
+    rx[11:14] = jnp.zeros((3,) + rx.shape[1:], F32)
     lax.fori_loop(0, 8, pack, 0)
 
-    pl.semaphore_wait(
-        barrier,
-        half + has_low.astype(jnp.int32) + has_high.astype(jnp.int32) + edge_low.astype(jnp.int32) + edge_high.astype(jnp.int32),
-    )
+    c_a = on(0, -DT * rho0_p)
+    c_b = on(1, -DT / rho0_p)
+    c_c = on(4, -DT)
+    fields_only = lane < 5 * NF
+
+    def advected(d, speed):
+        return c_a * left(d, 16) + c_b * left(d, 48) + c_c * right(d, 48) - (DT * speed) * d
+
+    def step_inner(x, carry):
+        d = A1 * (rx[4 + x] - rx[2 + x]) + A2 * (rx[5 + x] - rx[1 + x]) + A3 * (rx[6 + x] - rx[x])
+        r = rx[3 + x]
+        row = pl.ds(x, 1)
+        s = r * sg[row] + advected(d, mt[row]) + ex[x]
+        qs[x] = jnp.where(fields_only, s, r)
+        return carry
+
+    lax.fori_loop(0, 8, step_inner, 0)
+    hs[0] = -(A1 * rx[10] + A2 * rx[9] + A3 * rx[8])
+    hs[1] = -(A2 * rx[10] + A3 * rx[9])
+    hs[2] = -A3 * rx[10]
+    hs[3] = A3 * rx[3]
+    hs[4] = A2 * rx[3] + A3 * rx[4]
+    hs[5] = A1 * rx[3] + A2 * rx[4] + A3 * rx[5]
+
+    comes = (takes_low & has_low) | (takes_high & has_high)
+
+    @pl.when(jnp.logical_not(comes))
+    def _():
+        hr[...] = jnp.zeros_like(hr)
+
+    def count(flag):
+        return flag.astype(jnp.int32)
+
+    crossing = 1 + count(edge_low) + count(edge_high)
+    from_low = count(has_low) * (4 - count(takes_high))
+    from_high = count(has_high) * (4 - count(takes_low))
+    pl.semaphore_wait(barrier, half - 1 + from_low + from_high + count(second) * crossing)
+    pl.when(second)(lambda: greet_across(far))
 
     def remote(src, dst, send, recv, **where):
         return pltpu.make_async_remote_copy(
             src_ref=src, dst_ref=dst, send_sem=send, recv_sem=recv, device_id=where, device_id_type=MESH
         )
 
-    rx_up = remote(rx.at[8:11], rx.at[0:3], rx_send.at[0], rx_recv.at[0], gx=high)
-    rx_down = remote(rx.at[3:6], rx.at[11:14], rx_send.at[1], rx_recv.at[1], gx=low)
+    h_up = [remote(hs.at[j], hr.at[k], h_send.at[j], h_recv.at[k], gx=high, ta=base + j) for j in range(3)]
+    h_down = [
+        remote(hs.at[j], hr.at[k], h_send.at[j], h_recv.at[k], gx=low, ta=base + half - 6 + j) for j in range(3, 6)
+    ]
     fx_up = remote(fx.at[:, 8:11], fx.at[:, 0:3], ring_send.at[0], ring_recv.at[0], gx=high)
     fx_down = remote(fx.at[:, 3:6], fx.at[:, 11:14], ring_send.at[1], ring_recv.at[1], gx=low)
     th_down = remote(th_out.at[0], th_in.at[1], th_send.at[0], th_recv.at[1], ta=before)
     th_up = remote(th_out.at[1], th_in.at[0], th_send.at[1], th_recv.at[0], ta=after)
 
-    pl.when(has_high)(rx_up.start)
-    pl.when(has_low)(rx_down.start)
-    th_down.start()
-    th_up.start()
-    pl.when(has_high)(fx_up.start)
-    pl.when(has_low)(fx_down.start)
-
-    @pl.when(jnp.logical_not(has_low))
-    def _():
-        rx[0:3] = jnp.zeros((3,) + rx.shape[1:], F32)
-        fx[:, 0:3] = jnp.zeros((5, 3) + fx.shape[2:], F32)
-
-    @pl.when(jnp.logical_not(has_high))
-    def _():
-        rx[11:14] = jnp.zeros((3,) + rx.shape[1:], F32)
-        fx[:, 11:14] = jnp.zeros((5, 3) + fx.shape[2:], F32)
-
-    c_a = on(0, -DT * rho0_p)
-    c_b = on(1, -DT / rho0_p)
-    c_c = on(4, -DT)
-
-    pl.when(has_low)(rx_up.wait_recv)
-    pl.when(has_high)(rx_down.wait_recv)
-
-    def step_inner(x, carry):
-        d = A1 * (rx[4 + x] - rx[2 + x]) + A2 * (rx[5 + x] - rx[1 + x]) + A3 * (rx[6 + x] - rx[x])
-        r = rx[3 + x]
-        row = pl.ds(x, 1)
-        s = r * sg[row] - (DT * mt[row]) * d + ex[x]
-        s = s + c_a * left(d, 16) + c_b * left(d, 48) + c_c * right(d, 48)
-        qs[x] = jnp.where(lane < 80, s, r)
-        return carry
-
-    lax.fori_loop(0, 8, step_inner, 0)
-
+    def each(copies, method):
+        for copy in copies:
+            getattr(copy, method)()
+
+    pl.when(has_high)(lambda: each(h_up, "start"))
+    pl.when(has_low)(lambda: each(h_down, "start"))
     a_copies = []
     for i in range(1, half):
         there = lax.rem(k + i, half)
@@ -201,35 +236,36 @@
         a_copies.append(copy)
     gr[k] = qs[k]
 
-    th_up.wait_recv()
-    th_down.wait_recv()
-    damp_rho = -DT * rho0
-    damp_v = -DT / rho0
-
-    def local_part(x, carry):
-        for f in range(2):
-            ext[f, x, 5:8] = th_in[0, x, 3 * f : 3 * f + 3]
-            ext[f, x, 40:43] = th_in[1, x, 3 * f : 3 * f + 3]
-
-        def angular(f):
-            d = A1 * (ext[f, x, 9:41] - ext[f, x, 7:39]) + A2 * (ext[f, x, 10:42] - ext[f, x, 6:38])
-            return d + A3 * (ext[f, x, 11:43] - ext[f, x, 5:37])
-
-        keep = st[pl.ds(x, 1)]
-        around = inv_r * inv_dt
-        z = zr[x] + angular(0) * around
-        out[0, x] = fx[0, 3 + x] * keep + damp_rho * z
-        out[1, x] = fx[1, 3 + x] * keep
-        out[2, x] = fx[2, 3 + x] * keep + damp_v * dp[x]
-        out[3, x] = fx[3, 3 + x] * keep + damp_v * (angular(1) * around)
-        out[4, x] = fx[4, 3 + x] * keep - DT * z
-        return carry
-
-    lax.fori_loop(0, 8, local_part, 0)
+    pl.when(second | jnp.logical_not(edge_low))(th_down.start)
+    pl.when(second | jnp.logical_not(edge_high))(th_up.start)
+
+    def send_bulk():
+        pl.when(has_high)(fx_up.start)
+        pl.when(has_low)(fx_down.start)
+
+    pl.when(jnp.logical_not(second))(send_bulk)
+
+    @pl.when(jnp.logical_not(has_low))
+    def _():
+        fx[:, 0:3] = jnp.zeros((5, 3) + fx.shape[2:], F32)
+
+    @pl.when(jnp.logical_not(has_high))
+    def _():
+        fx[:, 11:14] = jnp.zeros((5, 3) + fx.shape[2:], F32)
 
     for copy in a_copies:
         copy.wait()
-    g = gr[...].reshape(8 * gr.shape[1], LANES)
+    for copy in small[4:]:
+        copy.wait()
+
+    @pl.when(comes)
+    def _():
+        for j in range(half):
+            remote(hs.at[0], hr.at[j], h_send.at[0], h_recv.at[j], gx=low).wait_recv()
+
+    speed = jnp.where(fields_only, mt[pl.ds(k, 1)], 0.0)
+    g = gr[...] + advected(hr[...], speed)
+    g = g.reshape(8 * gr.shape[1], LANES)
     highest = lax.Precision.HIGHEST
     coef = jnp.dot(forward[...], g, precision=highest, preferred_element_type=F32)
     zero_mode = jnp.sum(g, axis=0, keepdims=True)
@@ -263,7 +299,41 @@
             ps[5 * h + i] = jnp.where(lane < 80, c[8 * i : 8 * i + 8], spread)
     ps[10] = zero8
     across = remote(ps, pr, z_send, z_recv, ta=partner)
+
+    @pl.when(jnp.logical_not(second))
+    def _():
+        pl.semaphore_wait(far, crossing)
+        pl.when(edge_low)(th_down.start)
+        pl.when(edge_high)(th_up.start)
+
     across.start()
+    pl.when(second)(send_bulk)
+    th_up.wait_recv()
+    th_down.wait_recv()
+    damp_rho = -DT * rho0
+    damp_v = -DT / rho0
+
+    def local_part(x, carry):
+        for f in range(2):
+            ext[f, x, 5:8] = th_in[0, x, 3 * f : 3 * f + 3]
+            ext[f, x, 40:43] = th_in[1, x, 3 * f : 3 * f + 3]
+
+        def angular(f):
+            d = A1 * (ext[f, x, 9:41] - ext[f, x, 7:39]) + A2 * (ext[f, x, 10:42] - ext[f, x, 6:38])
+            return d + A3 * (ext[f, x, 11:43] - ext[f, x, 5:37])
+
+        keep = st[pl.ds(x, 1)]
+        around = inv_r * inv_dt
+        z = zr[x] + angular(0) * around
+        out[0, x] = fx[0, 3 + x] * keep + damp_rho * z
+        out[1, x] = fx[1, 3 + x] * keep
+        out[2, x] = fx[2, 3 + x] * keep + damp_v * dp[x]
+        out[3, x] = fx[3, 3 + x] * keep + damp_v * (angular(1) * around)
+        out[4, x] = fx[4, 3 + x] * keep - DT * z
+        return carry
+
+    lax.fori_loop(0, 8, local_part, 0)
+
     cuts = jnp.concatenate([cut[...]] * 8, axis=1)
     keep = jnp.where(row + 1 <= cuts, 2.0 / (n_ta * gr.shape[1]), 0.0)
     across.wait()
@@ -322,8 +392,8 @@
 
     lax.fori_loop(0, 8, merge, 0)
 
-    pl.when(has_high)(rx_up.wait_send)
-    pl.when(has_low)(rx_down.wait_send)
+    pl.when(has_high)(lambda: each(h_up, "wait_send"))
+    pl.when(has_low)(lambda: each(h_down, "wait_send"))
     pl.when(has_high)(fx_up.wait_send)
     pl.when(has_low)(fx_down.wait_send)
     th_down.wait_send()
@@ -350,10 +420,17 @@
         dma = pltpu.SemaphoreType.DMA
         return pl.pallas_call(
             functools.partial(body, n_gx, n_ta, 2.0 * math.pi / n_theta),
-            out_shape=jax.ShapeDtypeStruct(fields.shape, F32),
-            in_specs=[pl.BlockSpec(memory_space=pl.ANY)] + [vmem] * 6,
+            out_shape=pltpu.VMEM(fields.shape, F32),
+            in_specs=[pl.BlockSpec(memory_space=pltpu.HBM)] * 7,
             out_specs=vmem,
             scratch_shapes=[
+                pltpu.VMEM((nx, nr), F32),
+                pltpu.VMEM((1, nr), F32),
+                pltpu.VMEM((nx, nr), jnp.int32),
+                pltpu.VMEM((1, NF), jnp.int32),
+                pltpu.VMEM(forward.shape, F32),
+                pltpu.VMEM(inverse.shape, F32),
+                dma((6,)),
                 pltpu.VMEM((nf, nx + 6, nt, nr), F32),
                 pltpu.VMEM((2, nx, nt + 16, nr), F32),
                 pltpu.VMEM((nx + 6, nt, nr), F32),
@@ -362,6 +439,8 @@
                 pltpu.VMEM((nx, nt, nr), F32),
                 pltpu.VMEM((nx, nt, nr), F32),
                 pltpu.VMEM((nx, nt, nr), F32),
+                pltpu.VMEM((6, nt, nr), F32),
+                pltpu.VMEM((half, nt, nr), F32),
                 pltpu.VMEM((2, nx, 8, nr), F32),
                 pltpu.VMEM((2, nx, 8, nr), F32),
                 pltpu.VMEM((11, 8, nr), F32),
@@ -374,15 +453,16 @@
                 dma((2,)),
                 dma((2,)), dma((2,)),
                 dma((2,)), dma((2,)),
-                dma((2,)), dma((2,)),
+                dma((6,)), dma((half,)),
                 dma((half - 1,)), dma((half - 1,)),
                 dma, dma,
                 dma((half - 1,)), dma((half - 1,)),
+                pltpu.SemaphoreType.REGULAR,
             ],
             compiler_params=pltpu.CompilerParams(
-                collective_id=0, has_side_effects=True, vmem_limit_bytes=16 * 1024 * 1024
+                collective_id=0, has_side_effects=True, vmem_limit_bytes=40 * 1024 * 1024
             ),
-        )(
+        )(*[pltpu.with_memory_space_constraint(a, pltpu.HBM) for a in (
             fields,
             mean_axial,
             cycle_mean_density.reshape(1, nr),
@@ -390,7 +470,7 @@
             cycle_cutoff.reshape(1, NF),
             jnp.asarray(forward),
             jnp.asarray(inverse),
-        )
+        )])
 
     return jax.shard_map(
         on_device,

time: 48.7 us -> 39.2 us (0.80)
  local copies, waits for them, and re-layouts: 5.78 us -> 0.84 us
  Pallas kernels: 42.4 us -> 37.9 us
    unnamed x15 -> x1, local copies, waits for them, and re-layouts: 5.78 us -> 0.84 us
    pallas_call x1, Pallas kernels: 42.4 us -> 37.9 us  [on_device(): pl.pallas_call(functools.partial(body, n_gx, n_ta, 2.0 * math.pi / n_thet...]
where the time goes in v2:
time: 39.2 us; the launch traced here: 38.8 us
  Pallas kernels  37.9 us (97%)
  local copies, waits for them, and re-layouts  0.84 us (2%)
    pallas_call x1, Pallas kernels, on_device(): pl.pallas_call(functools.partial(body, n_gx, n_ta, 2.0 * math.pi / n_thet...  37.9 us
    unnamed x1, local copies, waits for them, and re-layouts  0.84 us

profile of v2, /device:TPU:24, one launch (start us, length us, event | category | flops | bytes accessed | tf_op | source)
XLA Modules:
  0.0 38.8 jit_solution(1161923572617509043)
XLA Ops:
  0.0 37.9 %shard_map.73 = f32[5,8,32,128]{3,2,1,0:T(8,128)S(1)} custom-call(f32[5,8,32,128]{3,2,1,0:T(8,128)} %fields.1, f32[8,128]{1,0:T(8,128)} %rest_0_.1, f32[1,128]{1,0:T(1,128)} %bitcast.2, s32[8,128]{1,0:T(8,128)} %rest_2_.1, s32[1,16]{1,0:T(1,128)} %bitcast.3, f32[128,256]{1,0:T(8,128)} %constant.4.clone.rest_4_, f32[256,128]{1,0:T(8,128)} %constant.5.clone.rest_5_), custom_call_target="tpu_custom_call" | custom-call | tf_op jit(solution)/shard_map/pallas_call | solution.py:421
  37.9 0.8 %copy.9 = f32[5,8,32,128]{3,2,1,0:T(8,128)} copy(f32[5,8,32,128]{3,2,1,0:T(8,128)S(1)} %shard_map.73) | data formatting | bytes 1310720

commit v3 on v2

--- a/solution.py
+++ b/solution.py
@@ -13,6 +13,7 @@
 PMLW = 12
 MODES = 64
 LANES = 128
+RUN = 8
 
 A1, A2, A3 = 0.770882380518, -0.166705904415, 0.020843142770
 DT = 0.1
@@ -41,7 +42,7 @@
 
 
 def body(
-    n_gx, n_ta, spacing,
+    n_gx, n_ta, run, spacing,
     fields, *rest,
 ):
     inputs, rest = rest[:6], rest[6:]
@@ -59,6 +60,7 @@
     ta = lax.axis_index("ta")
     k = lax.rem(ta, half)
     base = ta - k
+    other = lax.rem(base + half, n_ta)
     partner = lax.rem(ta + half, n_ta)
     after = lax.rem(ta + 1, n_ta)
     before = lax.rem(ta + n_ta - 1, n_ta)
@@ -68,10 +70,24 @@
     high = jnp.minimum(gx + 1, n_gx - 1)
     edge_low = k == 0
     edge_high = k == half - 1
+    farthest_first = sorted(range(1, half), key=lambda i: -min(i, half - i))
     second = ta >= half
+    first = jnp.logical_not(second)
+    cross_low = has_low & (lax.rem(gx, run) == 0)
+    cross_high = has_high & (lax.rem(gx, run) == run - 1)
+    ends = cross_low | cross_high
     mates = [base + lax.rem(k + i, half) for i in range(1, half)]
     takes_low = k < 3
     takes_high = k > half - 4
+
+    loads = [pltpu.make_async_copy(fields.at[f], fx.at[f, 3:11], load_sem.at[f]) for f in range(5)]
+    load_t = pltpu.make_async_copy(fields.at[3:5], ext.at[:, :, 8:40], load_sem.at[5])
+    for copy in loads:
+        copy.start()
+    small = [pltpu.make_async_copy(inputs[i], local[i], input_sem.at[i]) for i in range(6)]
+    for copy in small:
+        copy.start()
+    load_t.start()
 
     barrier = pltpu.get_barrier_semaphore()
 
@@ -85,25 +101,27 @@
 
     for mate in mates:
         greet(barrier, ta=mate)
-    pl.when(jnp.logical_not(second))(lambda: greet_across(barrier))
-    for exists, takes, there in ((has_low, takes_low, low), (has_high, takes_high, high)):
+    pl.when(first)(lambda: greet_across(barrier))
+    for exists, takes, cross, there in (
+        (has_low, takes_low, cross_low, low),
+        (has_high, takes_high, cross_high, high),
+    ):
 
         @pl.when(exists)
         def _():
-            greet(barrier, gx=there)
-
-            @pl.when(takes)
+            near_half = takes & (first | jnp.logical_not(cross))
+            pl.when(jnp.logical_not(near_half))(lambda: greet(barrier, gx=there))
+
+            @pl.when(near_half)
             def _():
-                for mate in mates:
-                    greet(barrier, gx=there, ta=mate)
-
-    load = pltpu.make_async_copy(fields, fx.at[:, 3:11], load_sem.at[0])
-    load.start()
-    load_t = pltpu.make_async_copy(fields.at[3:5], ext.at[:, :, 8:40], load_sem.at[1])
-    load_t.start()
-    small = [pltpu.make_async_copy(inputs[i], local[i], input_sem.at[i]) for i in range(6)]
-    for copy in small:
-        copy.start()
+                for j in range(half):
+                    greet(barrier, gx=there, ta=base + j)
+
+            @pl.when(takes & cross & first)
+            def _():
+                for j in range(half):
+                    greet(barrier, gx=there, ta=other + j)
+
     for copy in small[:4]:
         copy.wait()
 
@@ -140,8 +158,8 @@
         ghost = g_0 * f + g_u1 * ups[0] + g_u2 * ups[1] + g_d1 * dns[0] + g_d2 * dns[1]
         return d, ghost
 
-    load.wait()
-    load_t.wait()
+    for copy in loads:
+        copy.wait()
 
     def pack(x, carry):
         rho, u, v, w, p = (fx[f, 3 + x] for f in range(5))
@@ -159,15 +177,11 @@
         rx[3 + x] = r
         e = jnp.where(lane < 16, z, jnp.where(lane < 48, right(dpr, 32), right(z, 64)))
         ex[x] = e * c_e
-        for f in range(2):
-            th_out[0, x, 3 * f : 3 * f + 3] = ext[f, x, 8:11]
-            th_out[1, x, 3 * f : 3 * f + 3] = ext[f, x, 37:40]
-        return carry
-
-    th_out[...] = jnp.zeros_like(th_out)
+        return carry
+
     rx[0:3] = jnp.zeros((3,) + rx.shape[1:], F32)
     rx[11:14] = jnp.zeros((3,) + rx.shape[1:], F32)
-    lax.fori_loop(0, 8, pack, 0)
+    lax.fori_loop(0, 8, pack, 0, unroll=True)
 
     c_a = on(0, -DT * rho0_p)
     c_b = on(1, -DT / rho0_p)
@@ -185,7 +199,7 @@
         qs[x] = jnp.where(fields_only, s, r)
         return carry
 
-    lax.fori_loop(0, 8, step_inner, 0)
+    lax.fori_loop(0, 8, step_inner, 0, unroll=True)
     hs[0] = -(A1 * rx[10] + A2 * rx[9] + A3 * rx[8])
     hs[1] = -(A2 * rx[10] + A3 * rx[9])
     hs[2] = -A3 * rx[10]
@@ -193,18 +207,25 @@
     hs[4] = A2 * rx[3] + A3 * rx[4]
     hs[5] = A1 * rx[3] + A2 * rx[4] + A3 * rx[5]
 
-    comes = (takes_low & has_low) | (takes_high & has_high)
+    comes = (takes_low & has_low & (first | jnp.logical_not(cross_low))) | (
+        takes_high & has_high & (first | jnp.logical_not(cross_high))
+    )
+    comes_across = first & ((takes_low & cross_low) | (takes_high & cross_high))
 
     @pl.when(jnp.logical_not(comes))
     def _():
-        hr[...] = jnp.zeros_like(hr)
+        hr[0] = jnp.zeros(hr.shape[1:], F32)
+
+    @pl.when(jnp.logical_not(comes_across))
+    def _():
+        hr[1] = jnp.zeros(hr.shape[1:], F32)
 
     def count(flag):
         return flag.astype(jnp.int32)
 
     crossing = 1 + count(edge_low) + count(edge_high)
-    from_low = count(has_low) * (4 - count(takes_high))
-    from_high = count(has_high) * (4 - count(takes_low))
+    from_low = count(has_low) * (4 - count(takes_high & (first | jnp.logical_not(cross_low))))
+    from_high = count(has_high) * (4 - count(takes_low & (first | jnp.logical_not(cross_high))))
     pl.semaphore_wait(barrier, half - 1 + from_low + from_high + count(second) * crossing)
     pl.when(second)(lambda: greet_across(far))
 
@@ -213,10 +234,13 @@
             src_ref=src, dst_ref=dst, send_sem=send, recv_sem=recv, device_id=where, device_id_type=MESH
         )
 
-    h_up = [remote(hs.at[j], hr.at[k], h_send.at[j], h_recv.at[k], gx=high, ta=base + j) for j in range(3)]
-    h_down = [
-        remote(hs.at[j], hr.at[k], h_send.at[j], h_recv.at[k], gx=low, ta=base + half - 6 + j) for j in range(3, 6)
-    ]
+    def halo(j, there, target, way):
+        return remote(hs.at[j], hr.at[way, k], h_send.at[j], h_recv.at[way, k], gx=there, ta=target)
+
+    h_up = [halo(j, high, base + j, 0) for j in range(3)]
+    h_up_across = [halo(j, high, other + j, 1) for j in range(3)]
+    h_down = [halo(j, low, base + half - 6 + j, 0) for j in range(3, 6)]
+    h_down_across = [halo(j, low, other + half - 6 + j, 1) for j in range(3, 6)]
     fx_up = remote(fx.at[:, 8:11], fx.at[:, 0:3], ring_send.at[0], ring_recv.at[0], gx=high)
     fx_down = remote(fx.at[:, 3:6], fx.at[:, 11:14], ring_send.at[1], ring_recv.at[1], gx=low)
     th_down = remote(th_out.at[0], th_in.at[1], th_send.at[0], th_recv.at[1], ta=before)
@@ -226,24 +250,39 @@
         for copy in copies:
             getattr(copy, method)()
 
-    pl.when(has_high)(lambda: each(h_up, "start"))
-    pl.when(has_low)(lambda: each(h_down, "start"))
     a_copies = []
-    for i in range(1, half):
+    for i in farthest_first:
         there = lax.rem(k + i, half)
         copy = remote(qs.at[there], gr.at[k], a_send.at[i - 1], a_recv.at[i - 1], ta=base + there)
         copy.start()
         a_copies.append(copy)
+    pl.when(has_high & (first | jnp.logical_not(cross_high)))(lambda: each(h_up, "start"))
+    pl.when(has_low & (first | jnp.logical_not(cross_low)))(lambda: each(h_down, "start"))
+    pl.when(cross_high & second)(lambda: each(h_up_across, "start"))
+    pl.when(cross_low & second)(lambda: each(h_down_across, "start"))
     gr[k] = qs[k]
 
+    def pack_edges(x, carry):
+        for f in range(2):
+            th_out[0, x, 3 * f : 3 * f + 3] = ext[f, x, 8:11]
+            th_out[1, x, 3 * f : 3 * f + 3] = ext[f, x, 37:40]
+        return carry
+
+    load_t.wait()
+    th_out[...] = jnp.zeros_like(th_out)
+    lax.fori_loop(0, 8, pack_edges, 0)
     pl.when(second | jnp.logical_not(edge_low))(th_down.start)
     pl.when(second | jnp.logical_not(edge_high))(th_up.start)
 
-    def send_bulk():
-        pl.when(has_high)(fx_up.start)
-        pl.when(has_low)(fx_down.start)
-
-    pl.when(jnp.logical_not(second))(send_bulk)
+    near_low = has_low & jnp.logical_not(cross_low)
+    near_high = has_high & jnp.logical_not(cross_high)
+    near_low = has_low & jnp.logical_not(cross_low)
+    near_high = has_high & jnp.logical_not(cross_high)
+    middle = jnp.logical_not(ends)
+    pl.when(cross_high & first)(fx_up.start)
+    pl.when(near_high & cross_low & first)(fx_up.start)
+    pl.when(near_high & first & middle)(fx_up.start)
+    pl.when(near_low & first & middle)(fx_down.start)
 
     @pl.when(jnp.logical_not(has_low))
     def _():
@@ -253,26 +292,39 @@
     def _():
         fx[:, 11:14] = jnp.zeros((5, 3) + fx.shape[2:], F32)
 
-    for copy in a_copies:
-        copy.wait()
+    @pl.when(first)
+    def _():
+        pl.semaphore_wait(far, crossing)
+        pl.when(edge_low)(th_down.start)
+        pl.when(edge_high)(th_up.start)
+
+    each(a_copies, "wait_recv")
     for copy in small[4:]:
         copy.wait()
 
-    @pl.when(comes)
-    def _():
-        for j in range(half):
-            remote(hs.at[0], hr.at[j], h_send.at[0], h_recv.at[j], gx=low).wait_recv()
+    for way, flag in ((0, comes), (1, comes_across)):
+
+        @pl.when(flag)
+        def _():
+            for j in range(half):
+                remote(hs.at[0], hr.at[way, j], h_send.at[0], h_recv.at[way, j], gx=low).wait_recv()
 
     speed = jnp.where(fields_only, mt[pl.ds(k, 1)], 0.0)
-    g = gr[...] + advected(hr[...], speed)
-    g = g.reshape(8 * gr.shape[1], LANES)
+    rows = half * gr.shape[1]
+    parts = [gr[...], hr[0], hr[1]]
+    g = jnp.concatenate([part.reshape(rows, LANES) for part in parts], axis=1)
     highest = lax.Precision.HIGHEST
     coef = jnp.dot(forward[...], g, precision=highest, preferred_element_type=F32)
-    zero_mode = jnp.sum(g, axis=0, keepdims=True)
-    a_m, b_m = coef[:MODES], coef[MODES:]
     kappa = 2.0 * (A1 * forward[MODES:, 1:2] + A2 * forward[MODES:, 2:3] + A3 * forward[MODES:, 3:4])
     row = lax.broadcasted_iota(jnp.int32, (MODES, LANES), 0)
     sign = jnp.where(lax.rem(row, 2) == 1, 1.0, -1.0)
+    zero_mode = jnp.sum(g, axis=0, keepdims=True)
+    zero_mode = zero_mode[:, :LANES] + advected(zero_mode[:, LANES : 2 * LANES] + zero_mode[:, 2 * LANES :], speed)
+
+    def gathered(c):
+        return c[:, :LANES] + advected(c[:, LANES : 2 * LANES] + sign * c[:, 2 * LANES :], speed)
+
+    a_m, b_m = gathered(coef[:MODES]), gathered(coef[MODES:])
     around_p = -DT * inv_r_p * inv_dt
     t_r, t_p, t_w = on(0, around_p * rho0_p), on(4, around_p), on(3, around_p / rho0_p)
     three = lane < 3
@@ -300,43 +352,53 @@
     ps[10] = zero8
     across = remote(ps, pr, z_send, z_recv, ta=partner)
 
-    @pl.when(jnp.logical_not(second))
-    def _():
-        pl.semaphore_wait(far, crossing)
-        pl.when(edge_low)(th_down.start)
-        pl.when(edge_high)(th_up.start)
-
     across.start()
-    pl.when(second)(send_bulk)
+    pl.when(cross_low & first)(fx_down.start)
+    pl.when(near_low & cross_high & first)(fx_down.start)
+    damp_rho = -DT * rho0
+    damp_v = -DT / rho0
+
+    def local_part(x, carry):
+        keep = st[pl.ds(x, 1)]
+        z = zr[x]
+        out[0, x] = fx[0, 3 + x] * keep + damp_rho * z
+        out[1, x] = fx[1, 3 + x] * keep
+        out[2, x] = fx[2, 3 + x] * keep + damp_v * dp[x]
+        out[3, x] = fx[3, 3 + x] * keep
+        out[4, x] = fx[4, 3 + x] * keep - DT * z
+        return carry
+
+    lax.fori_loop(0, 8, local_part, 0)
+    pl.when(cross_low & second)(fx_down.start)
+    pl.when(cross_high & second)(fx_up.start)
+    pl.when(near_high & second & middle)(fx_up.start)
+    pl.when(near_low & second & middle)(fx_down.start)
+    pl.when(near_high & cross_low & second)(fx_up.start)
+    pl.when(near_low & cross_high & second)(fx_down.start)
     th_up.wait_recv()
     th_down.wait_recv()
-    damp_rho = -DT * rho0
-    damp_v = -DT / rho0
-
-    def local_part(x, carry):
+    around = inv_r * inv_dt
+
+    def angular_part(x, carry):
         for f in range(2):
             ext[f, x, 5:8] = th_in[0, x, 3 * f : 3 * f + 3]
             ext[f, x, 40:43] = th_in[1, x, 3 * f : 3 * f + 3]
 
         def angular(f):
             d = A1 * (ext[f, x, 9:41] - ext[f, x, 7:39]) + A2 * (ext[f, x, 10:42] - ext[f, x, 6:38])
-            return d + A3 * (ext[f, x, 11:43] - ext[f, x, 5:37])
-
-        keep = st[pl.ds(x, 1)]
-        around = inv_r * inv_dt
-        z = zr[x] + angular(0) * around
-        out[0, x] = fx[0, 3 + x] * keep + damp_rho * z
-        out[1, x] = fx[1, 3 + x] * keep
-        out[2, x] = fx[2, 3 + x] * keep + damp_v * dp[x]
-        out[3, x] = fx[3, 3 + x] * keep + damp_v * (angular(1) * around)
-        out[4, x] = fx[4, 3 + x] * keep - DT * z
-        return carry
-
-    lax.fori_loop(0, 8, local_part, 0)
+            return (d + A3 * (ext[f, x, 11:43] - ext[f, x, 5:37])) * around
+
+        d_w = angular(0)
+        out[0, x] = out[0, x] + damp_rho * d_w
+        out[3, x] = out[3, x] + damp_v * angular(1)
+        out[4, x] = out[4, x] - DT * d_w
+        return carry
+
+    lax.fori_loop(0, 8, angular_part, 0)
 
     cuts = jnp.concatenate([cut[...]] * 8, axis=1)
     keep = jnp.where(row + 1 <= cuts, 2.0 / (n_ta * gr.shape[1]), 0.0)
-    across.wait()
+    across.wait_recv()
 
     total = []
     for h, c in ((0, new_a), (1, new_b)):
@@ -354,7 +416,7 @@
     bs[...] = filtered.reshape(bs.shape)
 
     b_copies = []
-    for i in range(1, half):
+    for i in farthest_first:
         there = lax.rem(k + i, half)
         copy = remote(bs.at[there], br.at[k], b_send.at[i - 1], b_recv.at[i - 1], ta=base + there)
         copy.start()
@@ -381,8 +443,7 @@
 
     lax.fori_loop(0, 8, axial_part, 0)
 
-    for copy in b_copies:
-        copy.wait()
+    each(b_copies, "wait_recv")
 
     def merge(x, carry):
         t = br[x]
@@ -396,8 +457,7 @@
     pl.when(has_low)(lambda: each(h_down, "wait_send"))
     pl.when(has_high)(fx_up.wait_send)
     pl.when(has_low)(fx_down.wait_send)
-    th_down.wait_send()
-    th_up.wait_send()
+    each(a_copies + [across] + b_copies + [th_down, th_up], "wait_send")
 
 
 def tables(points, n_theta):
@@ -419,7 +479,7 @@
         half = n_ta // 2
         dma = pltpu.SemaphoreType.DMA
         return pl.pallas_call(
-            functools.partial(body, n_gx, n_ta, 2.0 * math.pi / n_theta),
+            functools.partial(body, n_gx, n_ta, RUN, 2.0 * math.pi / n_theta),
             out_shape=pltpu.VMEM(fields.shape, F32),
             in_specs=[pl.BlockSpec(memory_space=pltpu.HBM)] * 7,
             out_specs=vmem,
@@ -440,7 +500,7 @@
                 pltpu.VMEM((nx, nt, nr), F32),
                 pltpu.VMEM((nx, nt, nr), F32),
                 pltpu.VMEM((6, nt, nr), F32),
-                pltpu.VMEM((half, nt, nr), F32),
+                pltpu.VMEM((2, half, nt, nr), F32),
                 pltpu.VMEM((2, nx, 8, nr), F32),
                 pltpu.VMEM((2, nx, 8, nr), F32),
                 pltpu.VMEM((11, 8, nr), F32),
@@ -450,10 +510,10 @@
                 pltpu.VMEM((nx, nr), F32),
                 pltpu.VMEM((nx, nr), F32),
                 pltpu.VMEM((nx, nr), F32),
-                dma((2,)),
+                dma((6,)),
                 dma((2,)), dma((2,)),
                 dma((2,)), dma((2,)),
-                dma((6,)), dma((half,)),
+                dma((6,)), dma((2, half)),
                 dma((half - 1,)), dma((half - 1,)),
                 dma, dma,
                 dma((half - 1,)), dma((half - 1,)),

time: 39.2 us -> 35 us (0.89)
  Pallas kernels: 37.9 us -> 33.6 us
    pallas_call x1, Pallas kernels: 37.9 us -> 33.6 us  [on_device(): pl.pallas_call(functools.partial(body, n_gx, n_ta, RUN, 2.0 * math.pi / n...]
where the time goes in v3:
time: 35 us; the launch traced here: 34.5 us
  Pallas kernels  33.6 us (96%)
  local copies, waits for them, and re-layouts  0.84 us (2%)
    pallas_call x1, Pallas kernels, on_device(): pl.pallas_call(functools.partial(body, n_gx, n_ta, RUN, 2.0 * math.pi / n...  33.6 us
    unnamed x1, local copies, waits for them, and re-layouts  0.84 us

profile of v3, /device:TPU:24, one launch (start us, length us, event | category | flops | bytes accessed | tf_op | source)
XLA Modules:
  0.0 34.5 jit_solution(8443829106296660651)
XLA Ops:
  0.0 33.6 %shard_map.73 = f32[5,8,32,128]{3,2,1,0:T(8,128)S(1)} custom-call(f32[5,8,32,128]{3,2,1,0:T(8,128)} %fields.1, f32[8,128]{1,0:T(8,128)} %rest_0_.1, f32[1,128]{1,0:T(1,128)} %bitcast.2, s32[8,128]{1,0:T(8,128)} %rest_2_.1, s32[1,16]{1,0:T(1,128)} %bitcast.3, f32[128,256]{1,0:T(8,128)} %constant.4.clone.rest_4_, f32[256,128]{1,0:T(8,128)} %constant.5.clone.rest_5_), custom_call_target="tpu_custom_call" | custom-call | tf_op jit(solution)/shard_map/pallas_call | solution.py:481
  33.6 0.8 %copy.9 = f32[5,8,32,128]{3,2,1,0:T(8,128)} copy(f32[5,8,32,128]{3,2,1,0:T(8,128)S(1)} %shard_map.73) | data formatting | bytes 1310720

commit v4 on v3

--- a/solution.py
+++ b/solution.py
@@ -39,6 +39,18 @@
 
 def group(lane, g):
     return (lane >= NF * g) & (lane < NF * (g + 1))
+
+
+def narrow(x, lane):
+    last = x[..., 24:32, :]
+    first = jnp.where(lane < 80, x[..., 0:8, :], right(last, 80))
+    second = jnp.where(lane < 80, x[..., 8:16, :], right(last, 32))
+    return jnp.concatenate([first, second, x[..., 16:24, :]], axis=-2)
+
+
+def widen(x, lane):
+    last = jnp.where(lane < 48, left(x[..., 0:8, :], 80), left(x[..., 8:16, :], 32))
+    return jnp.concatenate([x, last], axis=-2)
 
 
 def body(
@@ -200,12 +212,18 @@
         return carry
 
     lax.fori_loop(0, 8, step_inner, 0, unroll=True)
-    hs[0] = -(A1 * rx[10] + A2 * rx[9] + A3 * rx[8])
-    hs[1] = -(A2 * rx[10] + A3 * rx[9])
-    hs[2] = -A3 * rx[10]
-    hs[3] = A3 * rx[3]
-    hs[4] = A2 * rx[3] + A3 * rx[4]
-    hs[5] = A1 * rx[3] + A2 * rx[4] + A3 * rx[5]
+    edge = [rx[x] for x in (3, 4, 5, 8, 9, 10)]
+    for j, combined in enumerate(
+        (
+            -(A1 * edge[5] + A2 * edge[4] + A3 * edge[3]),
+            -(A2 * edge[5] + A3 * edge[4]),
+            -A3 * edge[5],
+            A3 * edge[0],
+            A2 * edge[0] + A3 * edge[1],
+            A1 * edge[0] + A2 * edge[1] + A3 * edge[2],
+        )
+    ):
+        hs[j] = narrow(combined, lane)
 
     comes = (takes_low & has_low & (first | jnp.logical_not(cross_low))) | (
         takes_high & has_high & (first | jnp.logical_not(cross_high))
@@ -241,8 +259,14 @@
     h_up_across = [halo(j, high, other + j, 1) for j in range(3)]
     h_down = [halo(j, low, base + half - 6 + j, 0) for j in range(3, 6)]
     h_down_across = [halo(j, low, other + half - 6 + j, 1) for j in range(3, 6)]
-    fx_up = remote(fx.at[:, 8:11], fx.at[:, 0:3], ring_send.at[0], ring_recv.at[0], gx=high)
-    fx_down = remote(fx.at[:, 3:6], fx.at[:, 11:14], ring_send.at[1], ring_recv.at[1], gx=low)
+    def bulk(part, fs, way, src, dst, there):
+        return remote(
+            fx.at[fs, src : src + 3], fx.at[fs, dst : dst + 3], ring_send.at[way, part], ring_recv.at[way, part], gx=there
+        )
+
+    parts = ((0, pl.ds(0, 2)), (1, pl.ds(2, 3)))
+    fx_up = [bulk(part, fs, 0, 8, 0, high) for part, fs in parts]
+    fx_down = [bulk(part, fs, 1, 3, 11, low) for part, fs in parts]
     th_down = remote(th_out.at[0], th_in.at[1], th_send.at[0], th_recv.at[1], ta=before)
     th_up = remote(th_out.at[1], th_in.at[0], th_send.at[1], th_recv.at[0], ta=after)
 
@@ -279,10 +303,10 @@
     near_low = has_low & jnp.logical_not(cross_low)
     near_high = has_high & jnp.logical_not(cross_high)
     middle = jnp.logical_not(ends)
-    pl.when(cross_high & first)(fx_up.start)
-    pl.when(near_high & cross_low & first)(fx_up.start)
-    pl.when(near_high & first & middle)(fx_up.start)
-    pl.when(near_low & first & middle)(fx_down.start)
+    pl.when(cross_high & first)(lambda: each(fx_up, "start"))
+    pl.when(near_high & cross_low & first)(lambda: each(fx_up, "start"))
+    pl.when(near_high & first & middle)(lambda: each(fx_up, "start"))
+    pl.when(near_low & first & middle)(lambda: each(fx_down, "start"))
 
     @pl.when(jnp.logical_not(has_low))
     def _():
@@ -292,39 +316,12 @@
     def _():
         fx[:, 11:14] = jnp.zeros((5, 3) + fx.shape[2:], F32)
 
-    @pl.when(first)
-    def _():
-        pl.semaphore_wait(far, crossing)
-        pl.when(edge_low)(th_down.start)
-        pl.when(edge_high)(th_up.start)
-
-    each(a_copies, "wait_recv")
     for copy in small[4:]:
         copy.wait()
-
-    for way, flag in ((0, comes), (1, comes_across)):
-
-        @pl.when(flag)
-        def _():
-            for j in range(half):
-                remote(hs.at[0], hr.at[way, j], h_send.at[0], h_recv.at[way, j], gx=low).wait_recv()
-
     speed = jnp.where(fields_only, mt[pl.ds(k, 1)], 0.0)
-    rows = half * gr.shape[1]
-    parts = [gr[...], hr[0], hr[1]]
-    g = jnp.concatenate([part.reshape(rows, LANES) for part in parts], axis=1)
-    highest = lax.Precision.HIGHEST
-    coef = jnp.dot(forward[...], g, precision=highest, preferred_element_type=F32)
     kappa = 2.0 * (A1 * forward[MODES:, 1:2] + A2 * forward[MODES:, 2:3] + A3 * forward[MODES:, 3:4])
     row = lax.broadcasted_iota(jnp.int32, (MODES, LANES), 0)
     sign = jnp.where(lax.rem(row, 2) == 1, 1.0, -1.0)
-    zero_mode = jnp.sum(g, axis=0, keepdims=True)
-    zero_mode = zero_mode[:, :LANES] + advected(zero_mode[:, LANES : 2 * LANES] + zero_mode[:, 2 * LANES :], speed)
-
-    def gathered(c):
-        return c[:, :LANES] + advected(c[:, LANES : 2 * LANES] + sign * c[:, 2 * LANES :], speed)
-
-    a_m, b_m = gathered(coef[:MODES]), gathered(coef[MODES:])
     around_p = -DT * inv_r_p * inv_dt
     t_r, t_p, t_w = on(0, around_p * rho0_p), on(4, around_p), on(3, around_p / rho0_p)
     three = lane < 3
@@ -332,6 +329,34 @@
     h_p = jnp.where((lane >= 64) & (lane < 67), -DT, 0.0)
     h_v = jnp.where((lane >= 32) & (lane < 35), DT / rho0_p, 0.0)
 
+
+    @pl.when(first)
+    def _():
+        pl.semaphore_wait(far, crossing)
+        pl.when(edge_low)(th_down.start)
+        pl.when(edge_high)(th_up.start)
+
+    each(a_copies, "wait_recv")
+
+    for way, flag in ((0, comes), (1, comes_across)):
+
+        @pl.when(flag)
+        def _():
+            for j in range(half):
+                remote(hs.at[0], hr.at[way, j], h_send.at[0], h_recv.at[way, j], gx=low).wait_recv()
+
+    rows = half * gr.shape[1]
+    sources = [gr[...], widen(hr[0], lane), widen(hr[1], lane)]
+    g = jnp.concatenate([part.reshape(rows, LANES) for part in sources], axis=1)
+    highest = lax.Precision.HIGHEST
+    coef = jnp.dot(forward[...], g, precision=highest, preferred_element_type=F32)
+    zero_mode = jnp.sum(g, axis=0, keepdims=True)
+    zero_mode = zero_mode[:, :LANES] + advected(zero_mode[:, LANES : 2 * LANES] + zero_mode[:, 2 * LANES :], speed)
+
+    def gathered(c):
+        return c[:, :LANES] + advected(c[:, LANES : 2 * LANES] + sign * c[:, 2 * LANES :], speed)
+
+    a_m, b_m = gathered(coef[:MODES]), gathered(coef[MODES:])
     def turned(c):
         return t_r * left(c, 80) + t_p * left(c, 16) + t_w * left(c, 48)
 
@@ -353,8 +378,11 @@
     across = remote(ps, pr, z_send, z_recv, ta=partner)
 
     across.start()
-    pl.when(cross_low & first)(fx_down.start)
-    pl.when(near_low & cross_high & first)(fx_down.start)
+    pl.when(cross_low & first)(lambda: each(fx_down, "start"))
+    pl.when(near_low & cross_high & first)(lambda: each(fx_down, "start"))
+    pl.when(near_high & second & middle)(lambda: each(fx_up, "start"))
+    pl.when(near_low & second & middle)(lambda: each(fx_down, "start"))
+    pl.when(near_high & cross_low & second)(fx_up[0].start)
     damp_rho = -DT * rho0
     damp_v = -DT / rho0
 
@@ -369,12 +397,10 @@
         return carry
 
     lax.fori_loop(0, 8, local_part, 0)
-    pl.when(cross_low & second)(fx_down.start)
-    pl.when(cross_high & second)(fx_up.start)
-    pl.when(near_high & second & middle)(fx_up.start)
-    pl.when(near_low & second & middle)(fx_down.start)
-    pl.when(near_high & cross_low & second)(fx_up.start)
-    pl.when(near_low & cross_high & second)(fx_down.start)
+    pl.when(cross_low & second)(lambda: each(fx_down, "start"))
+    pl.when(near_high & cross_low & second)(fx_up[1].start)
+    pl.when(cross_high & second)(lambda: each(fx_up, "start"))
+    pl.when(near_low & cross_high & second)(lambda: each(fx_down, "start"))
     th_up.wait_recv()
     th_down.wait_recv()
     around = inv_r * inv_dt
@@ -395,6 +421,29 @@
         return carry
 
     lax.fori_loop(0, 8, angular_part, 0)
+    taps = ((1, A1), (2, A2), (3, A3))
+
+    def add_axial(x, terms):
+        def axial(f):
+            total = None
+            for weight, value in terms(f, x):
+                total = weight * value if total is None else total + weight * value
+            return total
+
+        along = DT * mean[x : x + 1]
+        d_u, d_p = axial(1), axial(4)
+        out[0, x] = out[0, x] - along * axial(0) + damp_rho * d_u
+        out[1, x] = out[1, x] - along * d_u + damp_v * d_p
+        out[2, x] = out[2, x] - along * axial(2)
+        out[3, x] = out[3, x] - along * axial(3)
+        out[4, x] = out[4, x] - along * d_p - DT * d_u
+
+    def own_layers(f, x):
+        above = [(a, fx[f, 3 + x + s]) for s, a in taps if x + s <= 7]
+        return above + [(-a, fx[f, 3 + x - s]) for s, a in taps if x - s >= 0]
+
+    for x in range(8):
+        add_axial(x, own_layers)
 
     cuts = jnp.concatenate([cut[...]] * 8, axis=1)
     keep = jnp.where(row + 1 <= cuts, 2.0 / (n_ta * gr.shape[1]), 0.0)
@@ -413,7 +462,7 @@
     both = jnp.concatenate(total, axis=0)
     mean_mode = (zero8 + pr[10])[0:1] * (1.0 / (n_ta * gr.shape[1]))
     filtered = jnp.dot(inverse[...], both, precision=highest, preferred_element_type=F32) + mean_mode
-    bs[...] = filtered.reshape(bs.shape)
+    bs[...] = narrow(filtered.reshape(half, -1, LANES), lane)
 
     b_copies = []
     for i in farthest_first:
@@ -423,40 +472,27 @@
         b_copies.append(copy)
     br[k] = bs[k]
 
-    pl.when(has_low)(fx_up.wait_recv)
-    pl.when(has_high)(fx_down.wait_recv)
-    inv_rho0 = 1.0 / rho0
-
-    def axial_part(x, carry):
-        def axial(f):
-            d = A1 * (fx[f, 4 + x] - fx[f, 2 + x]) + A2 * (fx[f, 5 + x] - fx[f, 1 + x])
-            return d + A3 * (fx[f, 6 + x] - fx[f, x])
-
-        along = DT * mean[pl.ds(x, 1)]
-        d_u, d_p = axial(1), axial(4)
-        out[0, x] = out[0, x] - along * axial(0) + damp_rho * d_u
-        out[1, x] = out[1, x] - along * d_u + damp_v * d_p
-        out[2, x] = out[2, x] - along * axial(2)
-        out[3, x] = out[3, x] - along * axial(3)
-        out[4, x] = out[4, x] - along * d_p - DT * d_u
-        return carry
-
-    lax.fori_loop(0, 8, axial_part, 0)
+    pl.when(has_low)(lambda: each(fx_up, "wait_recv"))
+    for x in range(3):
+        add_axial(x, lambda f, x: [(-a, fx[f, 3 + x - s]) for s, a in taps if x - s < 0])
+    pl.when(has_high)(lambda: each(fx_down, "wait_recv"))
+    for x in range(5, 8):
+        add_axial(x, lambda f, x: [(a, fx[f, 3 + x + s]) for s, a in taps if x + s > 7])
 
     each(b_copies, "wait_recv")
 
     def merge(x, carry):
-        t = br[x]
+        t = widen(br[x], lane)
         for f in range(5):
             out[f, x] = jnp.where(lane < NF, left(t, 16 * f) if f else t, out[f, x])
         return carry
 
-    lax.fori_loop(0, 8, merge, 0)
+    lax.fori_loop(0, 8, merge, 0, unroll=4)
 
     pl.when(has_high)(lambda: each(h_up, "wait_send"))
     pl.when(has_low)(lambda: each(h_down, "wait_send"))
-    pl.when(has_high)(fx_up.wait_send)
-    pl.when(has_low)(fx_down.wait_send)
+    pl.when(has_high)(lambda: each(fx_up, "wait_send"))
+    pl.when(has_low)(lambda: each(fx_down, "wait_send"))
     each(a_copies + [across] + b_copies + [th_down, th_up], "wait_send")
 
 
@@ -499,19 +535,19 @@
                 pltpu.VMEM((nx, nt, nr), F32),
                 pltpu.VMEM((nx, nt, nr), F32),
                 pltpu.VMEM((nx, nt, nr), F32),
-                pltpu.VMEM((6, nt, nr), F32),
-                pltpu.VMEM((2, half, nt, nr), F32),
+                pltpu.VMEM((6, nt - 8, nr), F32),
+                pltpu.VMEM((2, half, nt - 8, nr), F32),
                 pltpu.VMEM((2, nx, 8, nr), F32),
                 pltpu.VMEM((2, nx, 8, nr), F32),
                 pltpu.VMEM((11, 8, nr), F32),
                 pltpu.VMEM((11, 8, nr), F32),
-                pltpu.VMEM((nx, nt, nr), F32),
-                pltpu.VMEM((nx, nt, nr), F32),
+                pltpu.VMEM((nx, nt - 8, nr), F32),
+                pltpu.VMEM((nx, nt - 8, nr), F32),
                 pltpu.VMEM((nx, nr), F32),
                 pltpu.VMEM((nx, nr), F32),
                 pltpu.VMEM((nx, nr), F32),
                 dma((6,)),
-                dma((2,)), dma((2,)),
+                dma((2, 2)), dma((2, 2)),
                 dma((2,)), dma((2,)),
                 dma((6,)), dma((2, half)),
                 dma((half - 1,)), dma((half - 1,)),

time: 35 us -> 34.1 us (0.974); the launches traced: 34.5 us -> 34 us
  Pallas kernels: 33.6 us -> 33.1 us
    pallas_call x1, Pallas kernels: 33.6 us -> 33.1 us  [on_device(): pl.pallas_call(functools.partial(body, n_gx, n_ta, RUN, 2.0 * math.pi / n...]
where the time goes in v4:
time: 34.1 us; the launch traced here: 34 us
  Pallas kernels  33.1 us (97%)
  local copies, waits for them, and re-layouts  0.84 us (2%)
    pallas_call x1, Pallas kernels, on_device(): pl.pallas_call(functools.partial(body, n_gx, n_ta, RUN, 2.0 * math.pi / n...  33.1 us
    unnamed x1, local copies, waits for them, and re-layouts  0.84 us

profile of v4, /device:TPU:24, one launch (start us, length us, event | category | flops | bytes accessed | tf_op | source)
XLA Modules:
  0.0 34.0 jit_solution(8031765407271004716)
XLA Ops:
  0.0 33.1 %shard_map.73 = f32[5,8,32,128]{3,2,1,0:T(8,128)S(1)} custom-call(f32[5,8,32,128]{3,2,1,0:T(8,128)} %fields.1, f32[8,128]{1,0:T(8,128)} %rest_0_.1, f32[1,128]{1,0:T(1,128)} %bitcast.2, s32[8,128]{1,0:T(8,128)} %rest_2_.1, s32[1,16]{1,0:T(1,128)} %bitcast.3, f32[128,256]{1,0:T(8,128)} %constant.4.clone.rest_4_, f32[256,128]{1,0:T(8,128)} %constant.5.clone.rest_5_), custom_call_target="tpu_custom_call" | custom-call | tf_op jit(solution)/shard_map/pallas_call | solution.py:517
  33.1 0.8 %copy.9 = f32[5,8,32,128]{3,2,1,0:T(8,128)} copy(f32[5,8,32,128]{3,2,1,0:T(8,128)S(1)} %shard_map.73) | data formatting | bytes 1310720
